TPU v7x, 128 devices: a whole 4x4x4 slice. The times are simulated.
128 devices in a mesh: rep: 4 (over z_hi, core), fsdp: 32 (over y, x, z_lo).
Axes of the slice: x: 4, y: 4, z: 4 (z_hi: 2, z_lo: 2; z = z_hi * 2 + z_lo), core: 2. Of those that a mesh axis runs over, the one named last changes fastest.
Arguments:
- gradient: bfloat16 [25, 1024, 5120], P(None, ('rep', 'fsdp'))
- left_basis: bfloat16 [128, 1024, 1024], P(('rep', 'fsdp')), may hold values from -0.1875 to 0.1875
- right_basis: bfloat16 [128, 1024, 1024], P(('rep', 'fsdp')), may hold values from -0.1875 to 0.1875
- moment: bfloat16 [128, 1024, 1024], P(('rep', 'fsdp')), may hold values from -0.59765625 to 0.59765625
- second: float32 [128, 1024, 1024], P(('rep', 'fsdp')), may hold values from 0.01 to 1
- owners: int32 [128], replicated, may hold values from 0 to 125, as said below
Outputs:
- direction: bfloat16 [25, 1024, 5120], P(None, ('rep', 'fsdp'))
- new_moment: bfloat16 [128, 1024, 1024], P(('rep', 'fsdp'))
- new_second: float32 [128, 1024, 1024], P(('rep', 'fsdp'))
Inputs may be any that keep to these rules, and one draw needn't show every extreme that they name: `owners`: every block number 0 to 124 appears exactly once; the other 3 entries equal 125.
All inputs are finite; a program needn't handle non-finite values.
Results may differ from a plain program's by a relative error of at most 0.006.
Values may be sent and summed in bfloat16 or wider, within the bound.
No kernel may reach another device: no remote copies, remote signals or barrier semaphores. Data moves between devices by JAX's collectives and lax.ppermute only.
A program may use at most 128 MiB of HBM per device.

v0:
```python
import jax
import jax.numpy as jnp
from jax import lax
from jax.experimental import pallas as pl
from jax.experimental.pallas import tpu as pltpu
from jax.sharding import PartitionSpec as P

STEP = 10

decay_rate = 0.95
clip_rms = 0.5
epsilon_adam = 1e-08

AXES = ("rep", "fsdp")
TILE = 512
LANES = 128
MIB = 1024 * 1024


def block_place(block, col_blocks, width):
    mat = (block * (1024 // col_blocks + 1)) >> 10
    col = pl.multiple_of((block - mat * col_blocks) * width, width)
    return mat, col


def gather_kernel(owners_hbm, grad_hbm, out_ref, owners_ref, slot_of, grad, owners_sem, sems):
    mats, rows, cols = grad_hbm.shape
    slots = out_ref.shape[0]
    width = out_ref.shape[2] - LANES
    col_blocks = cols // width
    blocks = mats * col_blocks
    pieces = sems.shape[0]
    step = mats // pieces

    owners = pltpu.make_async_copy(owners_hbm, owners_ref, owners_sem)
    owners.start()
    loads = []
    for k in range(pieces):
        part = pl.ds(k * step, step)
        loads.append(pltpu.make_async_copy(grad_hbm.at[part], grad.at[part], sems.at[k]))
        loads[-1].start()

    owners.wait()

    def invert(s, spare):
        owner = owners_ref[s]
        slot_of[owner] = s
        shifted = (s,) + spare[:-1]
        return tuple(jnp.where(owner >= blocks, new, old) for new, old in zip(shifted, spare))

    spare = lax.fori_loop(0, slots, invert, (jnp.int32(0),) * (slots - blocks), unroll=16)
    for s in spare:
        out_ref[s, :, :width] = jnp.zeros((rows, width), jnp.bfloat16)

    def send(i, acc):
        for c in range(col_blocks):
            x = grad[i, :, c * width : (c + 1) * width]
            out_ref[slot_of[i * col_blocks + c], :, :width] = x
            x = x.astype(jnp.float32)
            x = x * x
            parts = [x[:, k * LANES : (k + 1) * LANES] for k in range(width // LANES)]
            while len(parts) > 1:
                parts = [p + q for p, q in zip(parts[::2], parts[1::2])]
            acc = acc + parts[0]
        return acc

    acc = jnp.zeros((rows, LANES), jnp.float32)
    for k in range(pieces):
        loads[k].wait()
        acc = lax.fori_loop(k * step, (k + 1) * step, send, acc)

    total = jnp.broadcast_to(jnp.sum(acc, axis=0, keepdims=True), (rows, LANES))
    high = total.astype(jnp.bfloat16).astype(jnp.float32)
    rest = jnp.where(high == jnp.inf, 0.0, total - high)
    middle = rest.astype(jnp.bfloat16).astype(jnp.float32)
    low = rest - middle
    row = lax.broadcasted_iota(jnp.int32, (rows, LANES), 0)
    note = jnp.where(row == 0, high, jnp.where(row == 1, middle, jnp.where(row == 2, low, 0.0)))
    out_ref[:, :, width:] = jnp.broadcast_to(note.astype(jnp.bfloat16)[None], (slots, rows, LANES))


def gather(owners, gradient, slots, width):
    mats, rows, _ = gradient.shape
    pieces = 5 if mats % 5 == 0 else 1
    table = pltpu.SMEM((slots,), jnp.int32)
    return pl.pallas_call(
        gather_kernel,
        out_shape=pltpu.VMEM((slots, rows, width + LANES), jnp.bfloat16),
        in_specs=[pl.BlockSpec(memory_space=pltpu.HBM)] * 2,
        out_specs=pl.BlockSpec(memory_space=pltpu.VMEM),
        scratch_shapes=[
            table,
            table,
            pltpu.VMEM(gradient.shape, jnp.bfloat16),
            pltpu.SemaphoreType.DMA,
            pltpu.SemaphoreType.DMA((pieces,)),
        ],
        compiler_params=pltpu.CompilerParams(vmem_limit_bytes=16 * MIB),
        cost_estimate=pl.CostEstimate(flops=10**11, bytes_accessed=10**8, transcendentals=0),
        name="gather_blocks",
    )(owners, gradient)


def place_kernel(owners_ref, rows_ref, out_ref, sem):
    slots, _, width = rows_ref.shape
    mats, _, cols = out_ref.shape
    col_blocks = cols // width
    blocks = mats * col_blocks

    def put(s, carry):
        owner = owners_ref[s]

        @pl.when(owner < blocks)
        def _():
            mat, col = block_place(owner, col_blocks, width)
            pltpu.make_async_copy(rows_ref.at[s], out_ref.at[mat, :, pl.ds(col, width)], sem).start()

        return carry

    lax.fori_loop(0, slots, put, 0, unroll=8)
    pltpu.make_async_copy(out_ref, out_ref, sem).wait()


def place(owners, rows, out_shape):
    return pl.pallas_call(
        place_kernel,
        out_shape=jax.ShapeDtypeStruct(out_shape, jnp.bfloat16),
        in_specs=[pl.BlockSpec(memory_space=pltpu.SMEM), pl.BlockSpec(memory_space=pltpu.VMEM)],
        out_specs=pl.BlockSpec(memory_space=pltpu.HBM),
        scratch_shapes=[pltpu.SemaphoreType.DMA],
        compiler_params=pltpu.CompilerParams(vmem_limit_bytes=16 * MIB),
        name="place_blocks",
    )(owners, rows)


def dot(a, b):
    return jnp.dot(a, b, preferred_element_type=jnp.float32)


def step_kernel(
    elements, g, r, l, m, s, u, nm_hbm, ns_hbm,
    lt, half, ratio, back, nm, ns, nm_sems, ns_sems,
):
    size = lt.shape[0]
    tiles = size // TILE

    def cols(j):
        return pl.ds(j * TILE, TILE)

    def tile_out(src, dst, sems, j):
        return pltpu.make_async_copy(src.at[:, cols(j)], dst.at[0, :, cols(j)], sems.at[j])

    total_sq = jnp.sum(g[:, size:].astype(jnp.float32), axis=(0, 1), keepdims=True)
    clip_factor = jnp.minimum(1.0, clip_rms * lax.rsqrt(total_sq / elements + 1e-06))
    correction = 1.0 - decay_rate**STEP

    for j in range(tiles):
        lt[:, cols(j)] = l[0, cols(j), :].T
    for j in range(tiles):
        half[:, cols(j)] = dot(g[:, :size], r[0, :, cols(j)]).astype(jnp.bfloat16)
    for j in range(tiles):
        rotated = clip_factor * dot(lt[...], half[:, cols(j)])
        scaled = (1.0 - decay_rate) * rotated
        first_mean = decay_rate * m[0, :, cols(j)].astype(jnp.float32) + scaled
        new_second = decay_rate * s[0, :, cols(j)] + scaled * rotated
        nm[:, cols(j)] = first_mean.astype(jnp.bfloat16)
        ns[:, cols(j)] = new_second
        root = new_second * lax.rsqrt(new_second)
        denominator = root + epsilon_adam * correction**0.5
        ratio[:, cols(j)] = (first_mean * correction**-0.5 / denominator).astype(jnp.bfloat16)
    for j in range(tiles):
        tile_out(nm, nm_hbm, nm_sems, j).start()
        tile_out(ns, ns_hbm, ns_sems, j).start()
    for j in range(tiles):
        back[:, cols(j)] = dot(l[0], ratio[:, cols(j)]).astype(jnp.bfloat16)
    for j in range(tiles):
        u[:, cols(j)] = lax.dot_general(
            back[...], r[0, cols(j), :], (((1,), (1,)), ((), ())), preferred_element_type=jnp.float32
        ).astype(jnp.bfloat16)
    for j in range(tiles):
        tile_out(nm, nm_hbm, nm_sems, j).wait()
        tile_out(ns, ns_hbm, ns_sems, j).wait()


def slot_step(elements, g, right, left, moment, second):
    size = g.shape[0]
    tiles = size // TILE
    low = pltpu.VMEM((size, size), jnp.bfloat16)
    wide = pltpu.VMEM((size, size), jnp.float32)
    vmem = pl.BlockSpec(memory_space=pltpu.VMEM)
    hbm = pl.BlockSpec(memory_space=pltpu.HBM)

    def kernel(*refs):
        step_kernel(elements, *refs)

    return pl.pallas_call(
        kernel,
        out_shape=(
            pltpu.VMEM((size, size), jnp.bfloat16),
            jax.ShapeDtypeStruct((1, size, size), jnp.bfloat16),
            jax.ShapeDtypeStruct((1, size, size), jnp.float32),
        ),
        in_specs=[vmem] * 5,
        out_specs=(vmem, hbm, hbm),
        scratch_shapes=[low, low, low, low, low, wide]
        + [pltpu.SemaphoreType.DMA((tiles,))] * 2,
        compiler_params=pltpu.CompilerParams(vmem_limit_bytes=36 * MIB),
        cost_estimate=pl.CostEstimate(flops=8 * size**3, bytes_accessed=24 * size**2, transcendentals=2 * size**2),
        name="slot_step",
    )(g, right, left, moment, second)


def exchange(x):
    return lax.all_to_all(x, AXES, split_axis=0, concat_axis=0, tiled=True)


def shards(gradient, left_basis, right_basis, moment, second, owners):
    group_size = lax.axis_size(AXES)
    matrices, row_count, col_count = gradient.shape
    block_size = left_basis.shape[1]
    element_count = matrices * row_count * col_count * group_size
    gradient = pltpu.with_memory_space_constraint(gradient, pltpu.HBM)

    sending = gather(pltpu.with_memory_space_constraint(owners, pltpu.HBM), gradient, group_size, block_size)
    arrived = exchange(sending)
    update, new_moment, new_second = slot_step(
        element_count, arrived.reshape(block_size, block_size + LANES),
        right_basis, left_basis, moment, second,
    )
    returned = exchange(update.reshape(group_size, row_count, block_size))
    direction = place(owners, returned, gradient.shape)
    return (direction, new_moment, new_second)


def solution(mesh):
    return jax.shard_map(
        shards,
        mesh=mesh,
        in_specs=(
            P(None, AXES, None),
            P(AXES, None, None),
            P(AXES, None, None),
            P(AXES, None, None),
            P(AXES, None, None),
            P(),
        ),
        out_specs=(
            P(None, AXES, None),
            P(AXES, None, None),
            P(AXES, None, None),
        ),
        check_vma=False,
    )
```

profile of v0, /device:TPU:1, one launch (start us, length us, event | category | flops | bytes accessed | tf_op | source)
XLA Modules:
  0.0 92.5 jit_solution(13364030611700829421)
XLA Ops:
  0.6 0.0 copy-start.2
  0.6 0.0 copy-start.3
  0.7 0.0 copy-start.4
  0.7 1.9 %gather_blocks.1 = bf16[128,8,1152]{2,1,0:T(8,128)(2,1)S(1)} custom-call(s32[128]{0:T(128)} %owners_ref.1, bf16[25,8,5120]{2,1,0:T(8,128)(2,1)} %grad_hbm.1), custom_call_target="tpu_custom_call" | custom-call | flops 99999997952 | bytes 100000000 | tf_op jit(solution)/shard_map/gather_blocks/pallas_call | solution.py:86
  2.5 0.0 copy-start.1
  2.5 44.7 %all_to_all.10 = bf16[128,8,1152]{2,1,0:T(8,128)(2,1)S(1)} all-to-all(bf16[128,8,1152]{2,1,0:T(8,128)(2,1)S(1)} %gather_blocks.1), channel_id=1, replica_groups=mesh['rep'=4,'fsdp'=32] {'rep','fsdp'}, dimensions={0} | all-to-all | bytes 4718592 | tf_op jit(solution)/shard_map/all_to_all | solution.py:214
  47.2 0.0 copy-done.2
  47.3 0.0 copy-done.3
  47.3 0.0 copy-done.4
  47.3 0.0 copy-done.1
  47.3 9.3 %slot_step.1 = (bf16[1024,1024]{1,0:T(8,128)(2,1)S(1)}, bf16[1,1024,1024]{2,1,0:T(8,128)(2,1)}, f32[1,1024,1024]{2,1,0:T(8,128)}) custom-call(bf16[1024,1152]{1,0:T(8,128)(2,1)S(1)} %bitcast.2, bf16[1,1024,1024]{2,1,0:T(8,128)(2,1)S(1)} %copy-done.2, bf16[1,1024,1024]{2,1,0:T(8,128)(2,1)S(1)} %copy-done.3, bf16[1,1024,1024]{2,1,0:T(8,128)(2,1)S(1)} %copy-done.4, ...), custom_call_target="tpu_custom_call" | custom-call | flops 8589934592 | bytes 25165824 | tf_op jit(solution)/shard_map/slot_step/pallas_call | solution.py:196
  56.6 0.0 copy-start
  56.6 34.0 %all_to_all.11.rows_ref = bf16[128,8,1024]{2,1,0:T(8,128)(2,1)S(1)} all-to-all(bf16[128,8,1024]{2,1,0:T(8,128)(2,1)S(1)} %bitcast.3), channel_id=1, replica_groups=mesh['rep'=4,'fsdp'=32] {'rep','fsdp'}, dimensions={0} | all-to-all | bytes 4194304 | tf_op jit(solution)/shard_map/all_to_all | solution.py:214
  90.6 0.0 copy-done
  90.6 1.8 %place_blocks.1 = bf16[25,8,5120]{2,1,0:T(8,128)(2,1)} custom-call(s32[128]{0:T(128)S(1)} %copy-done, bf16[128,8,1024]{2,1,0:T(8,128)(2,1)S(1)} %all_to_all.11.rows_ref), custom_call_target="tpu_custom_call" | custom-call | tf_op jit(solution)/shard_map/place_blocks/pallas_call | solution.py:125
Async XLA Ops:
  0.6 46.6 %copy-start.2 = (bf16[1,1024,1024]{2,1,0:T(8,128)(2,1)S(1)}, bf16[1,1024,1024]{2,1,0:T(8,128)(2,1)}, u32[]{:S(2)}) copy-start(bf16[1,1024,1024]{2,1,0:T(8,128)(2,1)} %refs_1_.1) | copy-start | bytes 6291460
  0.6 46.6 %copy-start.3 = (bf16[1,1024,1024]{2,1,0:T(8,128)(2,1)S(1)}, bf16[1,1024,1024]{2,1,0:T(8,128)(2,1)}, u32[]{:S(2)}) copy-start(bf16[1,1024,1024]{2,1,0:T(8,128)(2,1)} %refs_2_.1) | copy-start | bytes 6291460
  0.7 46.6 %copy-start.4 = (bf16[1,1024,1024]{2,1,0:T(8,128)(2,1)S(1)}, bf16[1,1024,1024]{2,1,0:T(8,128)(2,1)}, u32[]{:S(2)}) copy-start(bf16[1,1024,1024]{2,1,0:T(8,128)(2,1)} %refs_3_.1) | copy-start | bytes 6291460
  2.5 44.7 %copy-start.1 = (f32[1,1024,1024]{2,1,0:T(8,128)S(1)}, f32[1,1024,1024]{2,1,0:T(8,128)}, u32[]{:S(2)}) copy-start(f32[1,1024,1024]{2,1,0:T(8,128)} %refs_4_.1) | copy-start | bytes 12582916
  56.6 34.1 %copy-start = (s32[128]{0:T(128)S(1)}, s32[128]{0:T(128)}, u32[]{:S(2)}) copy-start(s32[128]{0:T(128)} %owners_ref.1) | copy-start | bytes 1540
where the time goes:
time: 92.6 us; the launch traced here: 92.5 us
  blocking collectives  78.8 us (85%)
  Pallas kernels  13 us (14%)
    all_to_all x2, blocking collectives, exchange(): return lax.all_to_all(x, AXES, split_axis=0, concat_axis=0, tiled=True)  78.8 us
    pallas_call x1, Pallas kernels, slot_step(): pl.pallas_call(kernel, out_shape=(pltpu.VMEM((size, size), jnp.bfloat16),...  9.31 us
    pallas_call x1, Pallas kernels, gather(): pl.pallas_call(gather_kernel, out_shape=pltpu.VMEM((slots, rows, width +...  1.85 us

commit v1 on v0

--- a/solution.py
+++ b/solution.py
@@ -12,7 +12,7 @@
 epsilon_adam = 1e-08
 
 AXES = ("rep", "fsdp")
-TILE = 512
+TILE = 1024
 LANES = 128
 MIB = 1024 * 1024
 

time: 92.6 us -> 92.6 us (level)
  no operation moved by 1% of the time
where the time goes in v1:
time: 92.6 us; the launch traced here: 92.5 us
  blocking collectives  78.8 us (85%)
  Pallas kernels  13 us (14%)
    all_to_all x2, blocking collectives, exchange(): return lax.all_to_all(x, AXES, split_axis=0, concat_axis=0, tiled=True)  78.8 us
    pallas_call x1, Pallas kernels, slot_step(): pl.pallas_call(kernel, out_shape=(pltpu.VMEM((size, size), jnp.bfloat16),...  9.35 us
    pallas_call x1, Pallas kernels, gather(): pl.pallas_call(gather_kernel, out_shape=pltpu.VMEM((slots, rows, width +...  1.85 us

profile of v1, /device:TPU:1, one launch (start us, length us, event | category | flops | bytes accessed | tf_op | source)
XLA Modules:
  0.0 92.5 jit_solution(33535893348447115)
XLA Ops:
  0.6 0.0 copy-start.2
  0.6 0.0 copy-start.3
  0.7 0.0 copy-start.4
  0.7 1.9 %gather_blocks.1 = bf16[128,8,1152]{2,1,0:T(8,128)(2,1)S(1)} custom-call(s32[128]{0:T(128)} %owners_ref.1, bf16[25,8,5120]{2,1,0:T(8,128)(2,1)} %grad_hbm.1), custom_call_target="tpu_custom_call" | custom-call | flops 99999997952 | bytes 100000000 | tf_op jit(solution)/shard_map/gather_blocks/pallas_call | solution.py:86
  2.5 0.0 copy-start.1
  2.5 44.7 %all_to_all.10 = bf16[128,8,1152]{2,1,0:T(8,128)(2,1)S(1)} all-to-all(bf16[128,8,1152]{2,1,0:T(8,128)(2,1)S(1)} %gather_blocks.1), channel_id=1, replica_groups=mesh['rep'=4,'fsdp'=32] {'rep','fsdp'}, dimensions={0} | all-to-all | bytes 4718592 | tf_op jit(solution)/shard_map/all_to_all | solution.py:214
  47.2 0.0 copy-done.2
  47.3 0.0 copy-done.3
  47.3 0.0 copy-done.4
  47.3 0.0 copy-done.1
  47.3 9.3 %slot_step.1 = (bf16[1024,1024]{1,0:T(8,128)(2,1)S(1)}, bf16[1,1024,1024]{2,1,0:T(8,128)(2,1)}, f32[1,1024,1024]{2,1,0:T(8,128)}) custom-call(bf16[1024,1152]{1,0:T(8,128)(2,1)S(1)} %bitcast.2, bf16[1,1024,1024]{2,1,0:T(8,128)(2,1)S(1)} %copy-done.2, bf16[1,1024,1024]{2,1,0:T(8,128)(2,1)S(1)} %copy-done.3, bf16[1,1024,1024]{2,1,0:T(8,128)(2,1)S(1)} %copy-done.4, ...), custom_call_target="tpu_custom_call" | custom-call | flops 8589934592 | bytes 25165824 | tf_op jit(solution)/shard_map/slot_step/pallas_call | solution.py:196
  56.6 0.0 copy-start
  56.6 34.1 %all_to_all.11.rows_ref = bf16[128,8,1024]{2,1,0:T(8,128)(2,1)S(1)} all-to-all(bf16[128,8,1024]{2,1,0:T(8,128)(2,1)S(1)} %bitcast.3), channel_id=1, replica_groups=mesh['rep'=4,'fsdp'=32] {'rep','fsdp'}, dimensions={0} | all-to-all | bytes 4194304 | tf_op jit(solution)/shard_map/all_to_all | solution.py:214
  90.7 0.0 copy-done
  90.7 1.8 %place_blocks.1 = bf16[25,8,5120]{2,1,0:T(8,128)(2,1)} custom-call(s32[128]{0:T(128)S(1)} %copy-done, bf16[128,8,1024]{2,1,0:T(8,128)(2,1)S(1)} %all_to_all.11.rows_ref), custom_call_target="tpu_custom_call" | custom-call | tf_op jit(solution)/shard_map/place_blocks/pallas_call | solution.py:125
Async XLA Ops:
  0.6 46.6 %copy-start.2 = (bf16[1,1024,1024]{2,1,0:T(8,128)(2,1)S(1)}, bf16[1,1024,1024]{2,1,0:T(8,128)(2,1)}, u32[]{:S(2)}) copy-start(bf16[1,1024,1024]{2,1,0:T(8,128)(2,1)} %refs_1_.1) | copy-start | bytes 6291460
  0.6 46.6 %copy-start.3 = (bf16[1,1024,1024]{2,1,0:T(8,128)(2,1)S(1)}, bf16[1,1024,1024]{2,1,0:T(8,128)(2,1)}, u32[]{:S(2)}) copy-start(bf16[1,1024,1024]{2,1,0:T(8,128)(2,1)} %refs_2_.1) | copy-start | bytes 6291460
  0.7 46.6 %copy-start.4 = (bf16[1,1024,1024]{2,1,0:T(8,128)(2,1)S(1)}, bf16[1,1024,1024]{2,1,0:T(8,128)(2,1)}, u32[]{:S(2)}) copy-start(bf16[1,1024,1024]{2,1,0:T(8,128)(2,1)} %refs_3_.1) | copy-start | bytes 6291460
  2.5 44.7 %copy-start.1 = (f32[1,1024,1024]{2,1,0:T(8,128)S(1)}, f32[1,1024,1024]{2,1,0:T(8,128)}, u32[]{:S(2)}) copy-start(f32[1,1024,1024]{2,1,0:T(8,128)} %refs_4_.1) | copy-start | bytes 12582916
  56.6 34.1 %copy-start = (s32[128]{0:T(128)S(1)}, s32[128]{0:T(128)}, u32[]{:S(2)}) copy-start(s32[128]{0:T(128)} %owners_ref.1) | copy-start | bytes 1540
